TPU v7x, 512 devices: a whole 4x8x8 slice. The times are simulated.
512 devices in a mesh: perm: 16 (over y, core), summa: 32 (over z, x).
Axes of the slice: x: 4, y: 8, z: 8, core: 2. Of those that a mesh axis runs over, the one named last changes fastest.
Arguments:
- amplitudes: bfloat16 [16, 1024, 1024], P('perm', None, 'summa'), may hold values from -6 to 6
- cycle_panels: bfloat16 [16, 128, 64, 1024], P('perm', None, 'summa'), may hold values from -0.75 to 0.75
- tile_mask: int32 [8, 2, 8, 8], replicated, may hold values 0 or 1
- panel_slot: int32 [16], replicated, may hold values from 0 to 15, each once
- window_blocks: int32 [4], replicated, may hold values from 0 to 7, as said below
- virt_energy: float32 [1024], replicated, may hold values from 0.5 to 3
- row_energy: float32 [8], replicated, may hold values from -2 to -0.5
- col_energy: float32 [64], P('summa'), may hold values from -2 to -0.5
Outputs:
- update: bfloat16 [1024, 8, 64, 1024], P('perm', None, 'summa')
Inputs may be any that keep to these rules, and one draw needn't show every extreme that they name: `panel_slot`: a permutation: each of the 16 slots holds exactly one panel. `window_blocks`: 4 distinct tile numbers in no particular order; tile 0 and tile 8 - 1 are always among them.
All inputs are finite; a program needn't handle non-finite values.
Results may differ from a plain program's by a relative error of at most 0.001.
Values may be sent and summed in bfloat16 or wider, within the bound.
No kernel may reach another device: no remote copies, remote signals or barrier semaphores. Data moves between devices by JAX's collectives and lax.ppermute only.
A program may use at most 64 MiB of HBM per device.

v0:
```python
import jax
import jax.numpy as jnp
from jax import lax
from jax.experimental import pallas as pl
from jax.experimental.pallas import tpu as pltpu
from jax.sharding import PartitionSpec as P

CORES, CHIPS_Z, CHIPS_X = 2, 8, 4
ORDER_Z, ORDER_X = (7, 3, 6, 2, 5, 1, 4, 0), (3, 1, 2, 0)
ALONG_Z = [[z * CHIPS_X + x for z in ORDER_Z] for x in range(CHIPS_X)]
ALONG_X = [[z * CHIPS_X + x for x in ORDER_X] for z in range(CHIPS_Z)]
MIB = 1024 * 1024
LANES, MXU = 128, 256


def gather_by_exchange(value, groups):
    count = len(groups[0])
    copies = jnp.broadcast_to(value[None], (count, *value.shape))
    return lax.all_to_all(copies, "summa", 0, 0, axis_index_groups=groups, tiled=True)


def interleave(pairs, count):
    to = lax.broadcasted_iota(jnp.int32, (pairs * count, pairs * count), 0)
    of = lax.broadcasted_iota(jnp.int32, (pairs * count, pairs * count), 1)
    return (of == (to % pairs) * count + to // pairs).astype(jnp.float32).astype(jnp.bfloat16)


def rows_kernel(mask, window, row_tile, tiles, out, rows):
    x_count, windows, occ_rows, c_local, lanes = tiles.shape
    half, width = rows.shape[0], x_count * c_local
    summed = lanes // half
    blocks = lax.axis_size("perm") // CORES
    for i in range(occ_rows):
        for w in range(windows):
            tile = jnp.concatenate([tiles[ORDER_X.index(x), w, i] for x in range(x_count)], axis=0)
            tile = tile.astype(jnp.float32).T
            for k in range(summed):
                keep = mask[((i * summed + k) * blocks + row_tile[0]) * blocks + window[w]].astype(
                    jnp.float32
                )
                rows[:, i, pl.ds((k * windows + w) * width, width)] = (
                    tile[k * half : (k + 1) * half] * keep
                )
    out[...] = rows[...].reshape(out.shape).astype(out.dtype)


def amplitude_rows(tile_mask, window, row_tile, tiles):
    x_count, windows, occ_rows, c_local, lanes = tiles.shape
    summed = tile_mask.shape[1]
    half, depth = lanes // summed, summed * windows * x_count * c_local
    smem = pl.BlockSpec(memory_space=pltpu.SMEM)
    return pl.pallas_call(
        rows_kernel,
        out_shape=jax.ShapeDtypeStruct((half * occ_rows, depth), jnp.bfloat16),
        in_specs=[smem, smem, smem, pl.BlockSpec(memory_space=pltpu.VMEM)],
        out_specs=pl.BlockSpec(memory_space=pltpu.VMEM),
        scratch_shapes=[
            pltpu.VMEM((half, occ_rows, depth), jnp.float32),
        ],
        compiler_params=pltpu.CompilerParams(vmem_limit_bytes=16 * MIB),
    )(tile_mask.reshape(-1), window, row_tile, tiles)


def contract_kernel(
    panel_slot, window, lhs, row_energy, col_energy, slots, out, panels, done, came, left
):
    row_count, depth = lhs.shape
    halves, count, cols, width, lanes = panels.shape
    windows = window.shape[0]
    summed = count // windows
    blocks = panel_slot.shape[0] // summed
    fetches = [
        [
            pltpu.make_async_copy(
                slots.at[panel_slot[k * blocks + window[w]], :, :, pl.ds(n * lanes, lanes)],
                panels.at[n, k * windows + w],
                came.at[n, k * windows + w],
            )
            for k in range(summed)
            for w in range(windows)
        ]
        for n in range(halves)
    ]
    for fetch in fetches[0]:
        fetch.start()
    together = MXU // cols
    order = interleave(cols, together)
    stores = []
    for n in range(halves):
        for fetch in fetches[n]:
            fetch.wait()
        for fetch in sum(fetches[n + 1 : n + 2], []):
            fetch.start()
        for first in range(0, lanes, MXU):
            here = n * lanes + first
            rounded = []
            for j in range(cols):
                term = jnp.dot(
                    lhs[...],
                    panels[n, :, j, :, pl.ds(first, MXU)].reshape(depth, MXU),
                    preferred_element_type=jnp.float32,
                )
                parts = []
                for part in range(MXU // LANES):
                    gap = row_energy[...] + col_energy[pl.ds(j, 1), pl.ds(here + part * LANES, LANES)]
                    guess = pl.reciprocal(gap, approx=True)
                    parts.append(
                        term[:, part * LANES : (part + 1) * LANES] * (guess * (2.0 - gap * guess))
                    )
                rounded.append(jnp.concatenate(parts, axis=1).astype(out.dtype))
            for m in range(0, row_count, together):
                apart = jnp.concatenate([value[m : m + together] for value in rounded], axis=0)
                mixed = jnp.dot(order, apart, preferred_element_type=jnp.float32).astype(out.dtype)
                for part in range(MXU // LANES):
                    flat = done.at[here // LANES + part].reshape(row_count * cols, LANES)
                    flat[pl.ds(m * cols, MXU), :] = mixed[:, part * LANES : (part + 1) * LANES]
            for part in range(here // LANES, here // LANES + MXU // LANES):
                stores.append(
                    pltpu.make_async_copy(
                        done.at[part], out.at[:, :, pl.ds(part * LANES, LANES)], left.at[part]
                    )
                )
                stores[-1].start()
    for store in stores:
        store.wait()


def contract(panel_slot, window, lhs, row_energy, col_energy, slots):
    row_count, depth = lhs.shape
    _, cols, width, width_virt = slots.shape
    count, parts, halves = depth // width, width_virt // LANES, width_virt // MXU
    smem, vmem = pl.BlockSpec(memory_space=pltpu.SMEM), pl.BlockSpec(memory_space=pltpu.VMEM)
    hbm = pl.BlockSpec(memory_space=pltpu.HBM)
    return pl.pallas_call(
        contract_kernel,
        out_shape=jax.ShapeDtypeStruct((row_count, cols, width_virt), jnp.bfloat16),
        in_specs=[smem] * 2 + [vmem] * 3 + [hbm],
        out_specs=hbm,
        scratch_shapes=[
            pltpu.VMEM((halves, count, cols, width, width_virt // halves), slots.dtype),
            pltpu.VMEM((parts, row_count, cols, LANES), jnp.bfloat16),
            pltpu.SemaphoreType.DMA((halves, count)),
            pltpu.SemaphoreType.DMA((parts,)),
        ],
        compiler_params=pltpu.CompilerParams(vmem_limit_bytes=24 * MIB),
    )(
        panel_slot,
        window,
        lhs,
        row_energy,
        col_energy,
        pltpu.with_memory_space_constraint(slots, pltpu.HBM),
    )


def body(
    amplitudes,
    cycle_panels,
    tile_mask,
    panel_slot,
    window_blocks,
    virt_energy,
    row_energy,
    col_energy,
):
    _, _, col_local, width_virt = cycle_panels.shape
    c_local = amplitudes.shape[2]
    occ_rows, occ_summed = tile_mask.shape[:2]
    perm_count = lax.axis_size("perm")
    a_local = amplitudes.shape[1] // perm_count
    p = lax.axis_index("perm")

    slots = lax.all_gather(jnp.swapaxes(cycle_panels[0], 0, 1), "perm", axis=0)

    blocks = jnp.swapaxes(amplitudes[0].T.reshape(c_local, perm_count, a_local), 0, 1)
    blocks = lax.all_to_all(blocks, "perm", 0, 0, tiled=True)
    blocks, virt_energy, row_energy = lax.optimization_barrier((blocks, virt_energy, row_energy))
    blocks = blocks.reshape(occ_rows, occ_summed, c_local, a_local)
    blocks = jnp.concatenate([blocks[:, k] for k in range(occ_summed)], axis=-1)
    row_virt = lax.dynamic_slice_in_dim(virt_energy, p * a_local, a_local)
    rows = row_virt[:, None] - row_energy[None, :]
    rows = jnp.broadcast_to(rows[..., None], (*rows.shape, LANES)).reshape(-1, LANES)
    columns = virt_energy[None, :] - col_energy[:, None]
    tiles = gather_by_exchange(blocks, ALONG_Z)
    place = CHIPS_Z - 1 - window_blocks
    place = (place << 1 | place >> 2) & (CHIPS_Z - 1)
    tiles = jnp.stack(
        [lax.dynamic_index_in_dim(tiles, place[w], 0, False) for w in range(place.shape[0])]
    )
    tiles = gather_by_exchange(tiles, ALONG_X)
    tiles, rows, columns = lax.optimization_barrier((tiles, rows, columns))
    lhs = amplitude_rows(tile_mask, window_blocks, (p >> 1).reshape(1), tiles)
    result = contract(panel_slot, window_blocks, lhs, rows, columns, slots)
    return result.reshape(a_local, occ_rows, col_local, width_virt)


def solution(mesh):
    in_specs = (
        P("perm", None, "summa"),
        P("perm", None, "summa", None),
        P(),
        P(),
        P(),
        P(),
        P(),
        P("summa"),
    )
    out_specs = P("perm", None, "summa", None)
    return jax.shard_map(body, mesh=mesh, in_specs=in_specs, out_specs=out_specs, check_vma=False)
```

profile of v0, /device:TPU:1, one launch (start us, length us, event | category | flops | bytes accessed | tf_op | source)
XLA Modules:
  0.0 88.5 jit_solution(2223236287619140426)
XLA Ops:
  6.5 0.0 copy-start.1
  6.6 0.0 all-gather.3.cloned.1.call-start
  6.6 2.0 %copy.22 = bf16[1,128,2,1024]{3,1,2,0:T(8,128)(2,1)} copy(bf16[1,128,2,1024]{3,2,1,0:T(2,128)(2,1)} %param.9) | data formatting | bytes 1048576 | tf_op args[1]
  8.6 0.0 all-gather.3.cloned.1.call-update
  8.6 1.0 %reshape.47 = bf16[32,16,64]{2,1,0:T(8,128)(2,1)S(1)} reshape(bf16[32,1024]{1,0:T(8,128)(2,1)} %bitcast.31) | data formatting | bytes 131072 | tf_op jit(solution)/shard_map/reshape | solution.py:175
  9.7 0.1 reshape.51
  9.8 17.1 %all_to_all.15 = bf16[16,2,1024]{2,1,0:T(2,128)(2,1)S(1)} all-to-all(bf16[16,2,1024]{2,1,0:T(2,128)(2,1)S(1)} %reshape.51), channel_id=1, replica_groups=mesh['perm'=16,'summa'=32] {'perm'}, dimensions={0} | all-to-all | bytes 131072 | tf_op jit(solution)/shard_map/all_to_all | solution.py:176
  27.0 0.1 reshape.52
  27.1 0.1 pad_maximum_fusion.1
  27.2 0.9 broadcast_in_dim.6
  28.1 11.3 %all-to-all-start.1 = ((bf16[8,8,32,128]{3,2,1,0:T(8,128)(2,1)}), bf16[8,8,32,128]{3,2,1,0:T(8,128)(2,1)S(1)}, u32[]{:S(2)}, u32[]{:S(2)}) async-start(bf16[8,8,32,128]{3,2,1,0:T(8,128)(2,1)} %broadcast_in_dim.6), calls=%async_computation.1 | async-start | bytes 1048576 | tf_op jit(solution)/shard_map/all_to_all | solution.py:19
  39.4 0.7 or_and_fusion
  40.1 0.7 fusion
  48.1 2.8 %all-to-all-done.1 = bf16[8,8,32,128]{3,2,1,0:T(8,128)(2,1)S(1)} async-done(((bf16[8,8,32,128]{3,2,1,0:T(8,128)(2,1)}), bf16[8,8,32,128]{3,2,1,0:T(8,128)(2,1)S(1)}, u32[]{:S(2)}, u32[]{:S(2)}) %all-to-all-start.1) | async-done | bytes 524320 | tf_op jit(solution)/shard_map/all_to_all | solution.py:19
  50.9 1.2 %broadcast_in_dim.7 = bf16[4,4,8,32,128]{4,3,2,1,0:T(8,128)(2,1)} broadcast(bf16[4,8,32,128]{3,2,1,0:T(8,128)(2,1)S(1)} %pad_maximum_fusion), dimensions={1,2,3,4} | broadcast | bytes 1310720 | tf_op jit(solution)/shard_map/broadcast_in_dim | solution.py:18
  52.1 6.0 %all-to-all-start.2 = ((bf16[4,4,8,32,128]{4,3,2,1,0:T(8,128)(2,1)}), bf16[4,4,8,32,128]{4,3,2,1,0:T(8,128)(2,1)S(1)}, u32[]{:S(2)}, u32[]{:S(2)}) async-start(bf16[4,4,8,32,128]{4,3,2,1,0:T(8,128)(2,1)} %broadcast_in_dim.7), calls=%async_computation.2 | async-start | bytes 2097152 | tf_op jit(solution)/shard_map/all_to_all | solution.py:19
  58.1 0.0 copy-done.2
  58.1 0.1 reshape.45.mask
  58.2 0.0 copy-done.3
  58.2 0.1 dynamic_slice.20
  58.3 0.1 sub.38
  58.3 0.1 sub.39
  58.4 0.0 copy-done.4
  58.5 0.1 sub.41
  58.6 0.0 copy-done.5
  58.6 0.1 broadcast_subtract_fusion.col_energy
  58.6 10.9 %all-to-all-done.2.tiles = bf16[4,4,8,32,128]{4,3,2,1,0:T(8,128)(2,1)S(1)} async-done(((bf16[4,4,8,32,128]{4,3,2,1,0:T(8,128)(2,1)}), bf16[4,4,8,32,128]{4,3,2,1,0:T(8,128)(2,1)S(1)}, u32[]{:S(2)}, u32[]{:S(2)}) %all-to-all-start.2) | async-done | bytes 1048608 | tf_op jit(solution)/shard_map/all_to_all | solution.py:19
  69.6 0.1 broadcast_in_dim.8.row_energy
  69.7 2.1 %shard_map.82.lhs = bf16[512,1024]{1,0:T(8,128)(2,1)S(1)} custom-call(s32[1024]{0:T(1024)S(1)} %reshape.45.mask, s32[4]{0:T(128)S(1)} %copy-done, s32[1]{0:T(128)} %bitcast.row_tile, bf16[4,4,8,32,128]{4,3,2,1,0:T(8,128)(2,1)S(1)} %all-to-all-done.2.tiles), custom_call_target="tpu_custom_call" | custom-call | tf_op jit(solution)/shard_map/pallas_call | solution.py:52
  71.8 1.9 %all-gather.3.cloned.1.call-done = bf16[32,128,1024]{2,1,0:T(8,128)(2,1)} async-done(((bf16[2,128,1024]{2,1,0:T(8,128)(2,1)}), bf16[32,128,1024]{2,1,0:T(8,128)(2,1)}) %all-gather.3.cloned.1.call-update) | async-done | bytes 8388624 | tf_op jit(solution)/shard_map/all_gather | solution.py:173
  73.7 0.0 copy-done.1
  73.7 7.9 %shard_map.83 = bf16[512,2,1024]{2,1,0:T(2,128)(2,1)} custom-call(s32[16]{0:T(128)S(1)} %copy-done.1, s32[4]{0:T(128)S(1)} %copy-done, bf16[512,1024]{1,0:T(8,128)(2,1)S(1)} %shard_map.82.lhs, f32[512,128]{1,0:T(8,128)S(1)} %broadcast_in_dim.8.row_energy, f32[2,1024]{1,0:T(2,128)S(1)} %broadcast_subtract_fusion.col_energy, bf16[16,2,128,1024]{3,2,1,0:T(8,128)(2,1)} %bitcast.27), custom_call_target="tpu_custom_call" | custom-call | tf_op jit(solution)/shard_map/pallas_call | solution.py:134
  (12 shorter events, 0.1 us)
Async XLA Ops:
  6.5 51.9 %copy-start.4 = (f32[8]{0:T(128)S(1)}, f32[8]{0:T(128)}, u32[]{:S(2)}) copy-start(f32[8]{0:T(128)} %param.14) | copy-start | bytes 100
  6.5 51.6 %copy-start.3 = (f32[1024]{0:T(1024)S(1)}, f32[1024]{0:T(1024)}, u32[]{:S(2)}) copy-start(f32[1024]{0:T(1024)} %param.13) | copy-start | bytes 12292
  6.5 63.2 %copy-start = (s32[4]{0:T(128)S(1)}, s32[4]{0:T(128)}, u32[]{:S(2)}) copy-start(s32[4]{0:T(128)} %window.3) | copy-start | bytes 52
  6.5 51.5 %copy-start.2 = (s32[8,2,8,8]{3,2,1,0:T(8,128)S(1)}, s32[8,2,8,8]{3,2,1,0:T(8,128)}, u32[]{:S(2)}) copy-start(s32[8,2,8,8]{3,2,1,0:T(8,128)} %param.10) | copy-start | bytes 12292
  6.5 52.0 %copy-start.5 = (f32[2]{0:T(128)S(1)}, f32[2]{0:T(128)}, u32[]{:S(2)}) copy-start(f32[2]{0:T(128)} %param.15) | copy-start | bytes 28
  6.5 67.1 %copy-start.1 = (s32[16]{0:T(128)S(1)}, s32[16]{0:T(128)}, u32[]{:S(2)}) copy-start(s32[16]{0:T(128)} %panel_slot.1) | copy-start | bytes 196
  6.6 67.1 %all-gather.3.cloned.1.call-start = ((), (), s32[]{:S(2)}) async-start(), calls=%async_computation.3 | async-start | bytes 8912896 | tf_op jit(solution)/shard_map/all_gather | solution.py:173
  28.1 22.8 %all-to-all-start.1 = ((bf16[8,8,32,128]{3,2,1,0:T(8,128)(2,1)}), bf16[8,8,32,128]{3,2,1,0:T(8,128)(2,1)S(1)}, u32[]{:S(2)}, u32[]{:S(2)}) async-start(bf16[8,8,32,128]{3,2,1,0:T(8,128)(2,1)} %broadcast_in_dim.6), calls=%async_computation.1 | async-start | bytes 1048576 | tf_op jit(solution)/shard_map/all_to_all | solution.py:19
  52.1 17.5 %all-to-all-start.2 = ((bf16[4,4,8,32,128]{4,3,2,1,0:T(8,128)(2,1)}), bf16[4,4,8,32,128]{4,3,2,1,0:T(8,128)(2,1)S(1)}, u32[]{:S(2)}, u32[]{:S(2)}) async-start(bf16[4,4,8,32,128]{4,3,2,1,0:T(8,128)(2,1)} %broadcast_in_dim.7), calls=%async_computation.2 | async-start | bytes 2097152 | tf_op jit(solution)/shard_map/all_to_all | solution.py:19
Sparse Core Ops, SparseCore 0:
  9.5 64.1 all-gather.2
where the time goes:
time: 89.5 us; the launch traced here: 88.5 us
  between operations  20.9 us (23%)
  starting transfers between devices  17.3 us (19%)
  blocking collectives  17.1 us (19%)
  waiting for transfers between devices  15.6 us (17%)
  Pallas kernels  10 us (11%)
  local copies, waits for them, and re-layouts  6.65 us (7%)
    all_to_all x2, starting transfers between devices, gather_by_exchange(): lax.all_to_all(copies, 'summa', 0, 0, axis_index_groups=groups, tiled=True)  17.3 us
    all_to_all x1, blocking collectives, body(): blocks = lax.all_to_all(blocks, 'perm', 0, 0, tiled=True)  17.1 us
    all_to_all x2, waiting for transfers between devices, gather_by_exchange(): lax.all_to_all(copies, 'summa', 0, 0, axis_index_groups=groups, tiled=True)  13.7 us
    pallas_call x1, Pallas kernels, contract(): pl.pallas_call(contract_kernel, out_shape=jax.ShapeDtypeStruct((row_count...  7.93 us
    unnamed x14, local copies, waits for them, and re-layouts  2.18 us
    pallas_call x1, Pallas kernels, amplitude_rows(): pl.pallas_call(rows_kernel, out_shape=jax.ShapeDtypeStruct((half * occ_ro...  2.08 us
    broadcast_in_dim x2, local copies, waits for them, and re-layouts, gather_by_exchange(): copies = jnp.broadcast_to(value[None], (count, *value.shape))  2.06 us
    all_gather x1, waiting for transfers between devices, body(): slots = lax.all_gather(jnp.swapaxes(cycle_panels[0], 0, 1), 'perm', axis=0)  1.88 us
  transfers between devices with their start and end apart: 3, of which 3 were waited for; matrix products, arithmetic and copies ran while one was open for 6% of the time, Pallas kernels for 2%

commit v1 on v0

--- a/solution.py
+++ b/solution.py
@@ -62,65 +62,72 @@
 
 
 def contract_kernel(
-    panel_slot, window, lhs, row_energy, col_energy, slots, out, panels, done, came, left
+    panel_slot, window, lhs, row_energy, col_energy, slots, out, panels, first, done, came, left
 ):
     row_count, depth = lhs.shape
-    halves, count, cols, width, lanes = panels.shape
+    cols, count, width, width_virt = panels.shape
     windows = window.shape[0]
     summed = count // windows
     blocks = panel_slot.shape[0] // summed
     fetches = [
-        [
-            pltpu.make_async_copy(
-                slots.at[panel_slot[k * blocks + window[w]], :, :, pl.ds(n * lanes, lanes)],
-                panels.at[n, k * windows + w],
-                came.at[n, k * windows + w],
-            )
-            for k in range(summed)
-            for w in range(windows)
-        ]
-        for n in range(halves)
+        pltpu.make_async_copy(
+            slots.at[panel_slot[k * blocks + window[w]], j],
+            panels.at[j, k * windows + w],
+            came.at[j, k * windows + w],
+        )
+        for j in range(cols)
+        for k in range(summed)
+        for w in range(windows)
     ]
-    for fetch in fetches[0]:
+    for fetch in fetches:
         fetch.start()
     together = MXU // cols
     order = interleave(cols, together)
+    steps = [(j, n) for j in range(cols) for n in range(0, width_virt, MXU)]
     stores = []
-    for n in range(halves):
-        for fetch in fetches[n]:
-            fetch.wait()
-        for fetch in sum(fetches[n + 1 : n + 2], []):
-            fetch.start()
-        for first in range(0, lanes, MXU):
-            here = n * lanes + first
-            rounded = []
-            for j in range(cols):
-                term = jnp.dot(
-                    lhs[...],
-                    panels[n, :, j, :, pl.ds(first, MXU)].reshape(depth, MXU),
-                    preferred_element_type=jnp.float32,
-                )
-                parts = []
-                for part in range(MXU // LANES):
-                    gap = row_energy[...] + col_energy[pl.ds(j, 1), pl.ds(here + part * LANES, LANES)]
-                    guess = pl.reciprocal(gap, approx=True)
-                    parts.append(
-                        term[:, part * LANES : (part + 1) * LANES] * (guess * (2.0 - gap * guess))
-                    )
-                rounded.append(jnp.concatenate(parts, axis=1).astype(out.dtype))
-            for m in range(0, row_count, together):
-                apart = jnp.concatenate([value[m : m + together] for value in rounded], axis=0)
-                mixed = jnp.dot(order, apart, preferred_element_type=jnp.float32).astype(out.dtype)
-                for part in range(MXU // LANES):
-                    flat = done.at[here // LANES + part].reshape(row_count * cols, LANES)
-                    flat[pl.ds(m * cols, MXU), :] = mixed[:, part * LANES : (part + 1) * LANES]
-            for part in range(here // LANES, here // LANES + MXU // LANES):
-                stores.append(
-                    pltpu.make_async_copy(
-                        done.at[part], out.at[:, :, pl.ds(part * LANES, LANES)], left.at[part]
-                    )
-                )
-                stores[-1].start()
+
+    def product(j, n):
+        if n == 0:
+            for fetch in fetches[j * count : (j + 1) * count]:
+                fetch.wait()
+        return jnp.dot(
+            lhs[...],
+            panels[j, :, :, pl.ds(n, MXU)].reshape(depth, MXU),
+            preferred_element_type=jnp.float32,
+        )
+
+    def divided(term, j, n):
+        parts = []
+        for part in range(0, MXU, LANES):
+            gap = row_energy[...] + col_energy[pl.ds(j, 1), pl.ds(n + part, LANES)]
+            guess = pl.reciprocal(gap, approx=True)
+            parts.append(term[:, part : part + LANES] * (guess * (2.0 - gap * guess)))
+        return jnp.concatenate(parts, axis=1).astype(out.dtype)
+
+    def finish(term, j, n):
+        value = divided(term, j, n)
+        if j < cols - 1:
+            first[j, :, pl.ds(n, MXU)] = value
+            return
+        for m in range(0, row_count, together):
+            apart = [first[before, pl.ds(m, together), pl.ds(n, MXU)] for before in range(cols - 1)]
+            apart = jnp.concatenate(apart + [value[m : m + together]], axis=0)
+            mixed = jnp.dot(order, apart, preferred_element_type=jnp.float32).astype(out.dtype)
+            for part in range(MXU // LANES):
+                flat = done.at[n // LANES + part].reshape(row_count * cols, LANES)
+                flat[pl.ds(m * cols, MXU), :] = mixed[:, part * LANES : (part + 1) * LANES]
+        for part in range(n // LANES, (n + MXU) // LANES):
+            store = pltpu.make_async_copy(
+                done.at[part], out.at[:, :, pl.ds(part * LANES, LANES)], left.at[part]
+            )
+            store.start()
+            stores.append(store)
+
+    term = product(*steps[0])
+    for now, later in zip(steps, steps[1:] + [None]):
+        ahead = product(*later) if later else None
+        finish(term, *now)
+        term = ahead
     for store in stores:
         store.wait()
 
@@ -128,7 +135,7 @@
 def contract(panel_slot, window, lhs, row_energy, col_energy, slots):
     row_count, depth = lhs.shape
     _, cols, width, width_virt = slots.shape
-    count, parts, halves = depth // width, width_virt // LANES, width_virt // MXU
+    count, parts = depth // width, width_virt // LANES
     smem, vmem = pl.BlockSpec(memory_space=pltpu.SMEM), pl.BlockSpec(memory_space=pltpu.VMEM)
     hbm = pl.BlockSpec(memory_space=pltpu.HBM)
     return pl.pallas_call(
@@ -137,9 +144,10 @@
         in_specs=[smem] * 2 + [vmem] * 3 + [hbm],
         out_specs=hbm,
         scratch_shapes=[
-            pltpu.VMEM((halves, count, cols, width, width_virt // halves), slots.dtype),
+            pltpu.VMEM((cols, count, width, width_virt), slots.dtype),
+            pltpu.VMEM((cols - 1, row_count, width_virt), jnp.bfloat16),
             pltpu.VMEM((parts, row_count, cols, LANES), jnp.bfloat16),
-            pltpu.SemaphoreType.DMA((halves, count)),
+            pltpu.SemaphoreType.DMA((cols, count)),
             pltpu.SemaphoreType.DMA((parts,)),
         ],
         compiler_params=pltpu.CompilerParams(vmem_limit_bytes=24 * MIB),

time: 89.5 us -> 88.4 us (0.988)
  Pallas kernels: 10 us -> 9.04 us
    pallas_call x1, Pallas kernels: 7.93 us -> 6.96 us  [contract(): pl.pallas_call(contract_kernel, out_shape=jax.ShapeDtypeStruct((row_count...]
where the time goes in v1:
time: 88.4 us; the launch traced here: 87.5 us
  between operations  20.9 us (24%)
  starting transfers between devices  17.3 us (20%)
  blocking collectives  17.1 us (19%)
  waiting for transfers between devices  15.6 us (18%)
  Pallas kernels  9.04 us (10%)
  local copies, waits for them, and re-layouts  6.65 us (8%)
    all_to_all x2, starting transfers between devices, gather_by_exchange(): lax.all_to_all(copies, 'summa', 0, 0, axis_index_groups=groups, tiled=True)  17.3 us
    all_to_all x1, blocking collectives, body(): blocks = lax.all_to_all(blocks, 'perm', 0, 0, tiled=True)  17.1 us
    all_to_all x2, waiting for transfers between devices, gather_by_exchange(): lax.all_to_all(copies, 'summa', 0, 0, axis_index_groups=groups, tiled=True)  13.7 us
    pallas_call x1, Pallas kernels, contract(): pl.pallas_call(contract_kernel, out_shape=jax.ShapeDtypeStruct((row_count...  6.96 us
    unnamed x14, local copies, waits for them, and re-layouts  2.18 us
    pallas_call x1, Pallas kernels, amplitude_rows(): pl.pallas_call(rows_kernel, out_shape=jax.ShapeDtypeStruct((half * occ_ro...  2.08 us
    broadcast_in_dim x2, local copies, waits for them, and re-layouts, gather_by_exchange(): copies = jnp.broadcast_to(value[None], (count, *value.shape))  2.06 us
    all_gather x1, waiting for transfers between devices, body(): slots = lax.all_gather(jnp.swapaxes(cycle_panels[0], 0, 1), 'perm', axis=0)  1.88 us
  transfers between devices with their start and end apart: 3, of which 3 were waited for; matrix products, arithmetic and copies ran while one was open for 6% of the time, Pallas kernels for 2%

profile of v1, /device:TPU:1, one launch (start us, length us, event | category | flops | bytes accessed | tf_op | source)
XLA Modules:
  0.0 87.5 jit_solution(7221730468690224166)
XLA Ops:
  6.5 0.0 copy-start.1
  6.6 0.0 all-gather.3.cloned.1.call-start
  6.6 2.0 %copy.22 = bf16[1,128,2,1024]{3,1,2,0:T(8,128)(2,1)} copy(bf16[1,128,2,1024]{3,2,1,0:T(2,128)(2,1)} %param.9) | data formatting | bytes 1048576 | tf_op args[1]
  8.6 0.0 all-gather.3.cloned.1.call-update
  8.6 1.0 %reshape.47 = bf16[32,16,64]{2,1,0:T(8,128)(2,1)S(1)} reshape(bf16[32,1024]{1,0:T(8,128)(2,1)} %bitcast.31) | data formatting | bytes 131072 | tf_op jit(solution)/shard_map/reshape | solution.py:183
  9.7 0.1 reshape.51
  9.8 17.1 %all_to_all.15 = bf16[16,2,1024]{2,1,0:T(2,128)(2,1)S(1)} all-to-all(bf16[16,2,1024]{2,1,0:T(2,128)(2,1)S(1)} %reshape.51), channel_id=1, replica_groups=mesh['perm'=16,'summa'=32] {'perm'}, dimensions={0} | all-to-all | bytes 131072 | tf_op jit(solution)/shard_map/all_to_all | solution.py:184
  27.0 0.1 reshape.52
  27.1 0.1 pad_maximum_fusion.1
  27.2 0.9 %broadcast_in_dim.6 = bf16[8,8,32,128]{3,2,1,0:T(8,128)(2,1)} broadcast(bf16[8,32,128]{2,1,0:T(8,128)(2,1)S(1)} %pad_maximum_fusion.1), dimensions={1,2,3} | broadcast | bytes 589824 | tf_op jit(solution)/shard_map/broadcast_in_dim | solution.py:18
  28.1 11.3 %all-to-all-start.1 = ((bf16[8,8,32,128]{3,2,1,0:T(8,128)(2,1)}), bf16[8,8,32,128]{3,2,1,0:T(8,128)(2,1)S(1)}, u32[]{:S(2)}, u32[]{:S(2)}) async-start(bf16[8,8,32,128]{3,2,1,0:T(8,128)(2,1)} %broadcast_in_dim.6), calls=%async_computation.1 | async-start | bytes 1048576 | tf_op jit(solution)/shard_map/all_to_all | solution.py:19
  39.4 0.7 or_and_fusion
  40.1 0.7 fusion
  48.1 2.8 %all-to-all-done.1 = bf16[8,8,32,128]{3,2,1,0:T(8,128)(2,1)S(1)} async-done(((bf16[8,8,32,128]{3,2,1,0:T(8,128)(2,1)}), bf16[8,8,32,128]{3,2,1,0:T(8,128)(2,1)S(1)}, u32[]{:S(2)}, u32[]{:S(2)}) %all-to-all-start.1) | async-done | bytes 524320 | tf_op jit(solution)/shard_map/all_to_all | solution.py:19
  50.9 1.2 %broadcast_in_dim.7 = bf16[4,4,8,32,128]{4,3,2,1,0:T(8,128)(2,1)} broadcast(bf16[4,8,32,128]{3,2,1,0:T(8,128)(2,1)S(1)} %pad_maximum_fusion), dimensions={1,2,3,4} | broadcast | bytes 1310720 | tf_op jit(solution)/shard_map/broadcast_in_dim | solution.py:18
  52.1 6.0 %all-to-all-start.2 = ((bf16[4,4,8,32,128]{4,3,2,1,0:T(8,128)(2,1)}), bf16[4,4,8,32,128]{4,3,2,1,0:T(8,128)(2,1)S(1)}, u32[]{:S(2)}, u32[]{:S(2)}) async-start(bf16[4,4,8,32,128]{4,3,2,1,0:T(8,128)(2,1)} %broadcast_in_dim.7), calls=%async_computation.2 | async-start | bytes 2097152 | tf_op jit(solution)/shard_map/all_to_all | solution.py:19
  58.1 0.0 copy-done.2
  58.1 0.1 reshape.45.mask
  58.2 0.0 copy-done.3
  58.2 0.1 dynamic_slice.20
  58.3 0.1 sub.38
  58.3 0.1 sub.39
  58.4 0.0 copy-done.4
  58.5 0.1 sub.41
  58.6 0.0 copy-done.5
  58.6 0.1 broadcast_subtract_fusion.col_energy
  58.6 10.9 %all-to-all-done.2.tiles = bf16[4,4,8,32,128]{4,3,2,1,0:T(8,128)(2,1)S(1)} async-done(((bf16[4,4,8,32,128]{4,3,2,1,0:T(8,128)(2,1)}), bf16[4,4,8,32,128]{4,3,2,1,0:T(8,128)(2,1)S(1)}, u32[]{:S(2)}, u32[]{:S(2)}) %all-to-all-start.2) | async-done | bytes 1048608 | tf_op jit(solution)/shard_map/all_to_all | solution.py:19
  69.6 0.1 broadcast_in_dim.8.row_energy
  69.7 2.1 %shard_map.82.lhs = bf16[512,1024]{1,0:T(8,128)(2,1)S(1)} custom-call(s32[1024]{0:T(1024)S(1)} %reshape.45.mask, s32[4]{0:T(128)S(1)} %copy-done, s32[1]{0:T(128)} %bitcast.row_tile, bf16[4,4,8,32,128]{4,3,2,1,0:T(8,128)(2,1)S(1)} %all-to-all-done.2.tiles), custom_call_target="tpu_custom_call" | custom-call | tf_op jit(solution)/shard_map/pallas_call | solution.py:52
  71.8 1.9 %all-gather.3.cloned.1.call-done = bf16[32,128,1024]{2,1,0:T(8,128)(2,1)} async-done(((bf16[2,128,1024]{2,1,0:T(8,128)(2,1)}), bf16[32,128,1024]{2,1,0:T(8,128)(2,1)}) %all-gather.3.cloned.1.call-update) | async-done | bytes 8388624 | tf_op jit(solution)/shard_map/all_gather | solution.py:181
  73.7 0.0 copy-done.1
  73.7 7.0 %shard_map.83 = bf16[512,2,1024]{2,1,0:T(2,128)(2,1)} custom-call(s32[16]{0:T(128)S(1)} %copy-done.1, s32[4]{0:T(128)S(1)} %copy-done, bf16[512,1024]{1,0:T(8,128)(2,1)S(1)} %shard_map.82.lhs, f32[512,128]{1,0:T(8,128)S(1)} %broadcast_in_dim.8.row_energy, f32[2,1024]{1,0:T(2,128)S(1)} %broadcast_subtract_fusion.col_energy, bf16[16,2,128,1024]{3,2,1,0:T(8,128)(2,1)} %bitcast.27), custom_call_target="tpu_custom_call" | custom-call | tf_op jit(solution)/shard_map/pallas_call | solution.py:141
  (12 shorter events, 0.1 us)
Async XLA Ops:
  6.5 51.9 %copy-start.4 = (f32[8]{0:T(128)S(1)}, f32[8]{0:T(128)}, u32[]{:S(2)}) copy-start(f32[8]{0:T(128)} %param.14) | copy-start | bytes 100
  6.5 51.6 %copy-start.3 = (f32[1024]{0:T(1024)S(1)}, f32[1024]{0:T(1024)}, u32[]{:S(2)}) copy-start(f32[1024]{0:T(1024)} %param.13) | copy-start | bytes 12292
  6.5 63.2 %copy-start = (s32[4]{0:T(128)S(1)}, s32[4]{0:T(128)}, u32[]{:S(2)}) copy-start(s32[4]{0:T(128)} %window.3) | copy-start | bytes 52
  6.5 51.5 %copy-start.2 = (s32[8,2,8,8]{3,2,1,0:T(8,128)S(1)}, s32[8,2,8,8]{3,2,1,0:T(8,128)}, u32[]{:S(2)}) copy-start(s32[8,2,8,8]{3,2,1,0:T(8,128)} %param.10) | copy-start | bytes 12292
  6.5 52.0 %copy-start.5 = (f32[2]{0:T(128)S(1)}, f32[2]{0:T(128)}, u32[]{:S(2)}) copy-start(f32[2]{0:T(128)} %param.15) | copy-start | bytes 28
  6.5 67.1 %copy-start.1 = (s32[16]{0:T(128)S(1)}, s32[16]{0:T(128)}, u32[]{:S(2)}) copy-start(s32[16]{0:T(128)} %panel_slot.1) | copy-start | bytes 196
  6.6 67.1 %all-gather.3.cloned.1.call-start = ((), (), s32[]{:S(2)}) async-start(), calls=%async_computation.3 | async-start | bytes 8912896 | tf_op jit(solution)/shard_map/all_gather | solution.py:181
  28.1 22.8 %all-to-all-start.1 = ((bf16[8,8,32,128]{3,2,1,0:T(8,128)(2,1)}), bf16[8,8,32,128]{3,2,1,0:T(8,128)(2,1)S(1)}, u32[]{:S(2)}, u32[]{:S(2)}) async-start(bf16[8,8,32,128]{3,2,1,0:T(8,128)(2,1)} %broadcast_in_dim.6), calls=%async_computation.1 | async-start | bytes 1048576 | tf_op jit(solution)/shard_map/all_to_all | solution.py:19
  52.1 17.5 %all-to-all-start.2 = ((bf16[4,4,8,32,128]{4,3,2,1,0:T(8,128)(2,1)}), bf16[4,4,8,32,128]{4,3,2,1,0:T(8,128)(2,1)S(1)}, u32[]{:S(2)}, u32[]{:S(2)}) async-start(bf16[4,4,8,32,128]{4,3,2,1,0:T(8,128)(2,1)} %broadcast_in_dim.7), calls=%async_computation.2 | async-start | bytes 2097152 | tf_op jit(solution)/shard_map/all_to_all | solution.py:19
Sparse Core Ops, SparseCore 0:
  9.5 64.1 all-gather.2

commit v2 on v1

--- a/solution.py
+++ b/solution.py
@@ -79,7 +79,7 @@
         for k in range(summed)
         for w in range(windows)
     ]
-    for fetch in fetches:
+    for fetch in fetches[:count]:
         fetch.start()
     together = MXU // cols
     order = interleave(cols, together)
@@ -90,6 +90,8 @@
         if n == 0:
             for fetch in fetches[j * count : (j + 1) * count]:
                 fetch.wait()
+            for fetch in fetches[(j + 1) * count : (j + 2) * count]:
+                fetch.start()
         return jnp.dot(
             lhs[...],
             panels[j, :, :, pl.ds(n, MXU)].reshape(depth, MXU),

time: 88.4 us -> 88.7 us (level)
  no operation moved by 1% of the time
where the time goes in v2:
time: 88.7 us; the launch traced here: 87.7 us
  between operations  20.9 us (24%)
  starting transfers between devices  17.3 us (20%)
  blocking collectives  17.1 us (19%)
  waiting for transfers between devices  15.6 us (18%)
  Pallas kernels  9.27 us (10%)
  local copies, waits for them, and re-layouts  6.65 us (7%)
    all_to_all x2, starting transfers between devices, gather_by_exchange(): lax.all_to_all(copies, 'summa', 0, 0, axis_index_groups=groups, tiled=True)  17.3 us
    all_to_all x1, blocking collectives, body(): blocks = lax.all_to_all(blocks, 'perm', 0, 0, tiled=True)  17.1 us
    all_to_all x2, waiting for transfers between devices, gather_by_exchange(): lax.all_to_all(copies, 'summa', 0, 0, axis_index_groups=groups, tiled=True)  13.7 us
    pallas_call x1, Pallas kernels, contract(): pl.pallas_call(contract_kernel, out_shape=jax.ShapeDtypeStruct((row_count...  7.19 us
    unnamed x14, local copies, waits for them, and re-layouts  2.18 us
    pallas_call x1, Pallas kernels, amplitude_rows(): pl.pallas_call(rows_kernel, out_shape=jax.ShapeDtypeStruct((half * occ_ro...  2.08 us
    broadcast_in_dim x2, local copies, waits for them, and re-layouts, gather_by_exchange(): copies = jnp.broadcast_to(value[None], (count, *value.shape))  2.06 us
    all_gather x1, waiting for transfers between devices, body(): slots = lax.all_gather(jnp.swapaxes(cycle_panels[0], 0, 1), 'perm', axis=0)  1.88 us
  transfers between devices with their start and end apart: 3, of which 3 were waited for; matrix products, arithmetic and copies ran while one was open for 6% of the time, Pallas kernels for 2%

profile of v2, /device:TPU:1, one launch (start us, length us, event | category | flops | bytes accessed | tf_op | source)
XLA Modules:
  0.0 87.7 jit_solution(16850226338862930412)
XLA Ops:
  6.5 0.0 copy-start.1
  6.6 0.0 all-gather.3.cloned.1.call-start
  6.6 2.0 %copy.22 = bf16[1,128,2,1024]{3,1,2,0:T(8,128)(2,1)} copy(bf16[1,128,2,1024]{3,2,1,0:T(2,128)(2,1)} %param.9) | data formatting | bytes 1048576 | tf_op args[1]
  8.6 0.0 all-gather.3.cloned.1.call-update
  8.6 1.0 %reshape.47 = bf16[32,16,64]{2,1,0:T(8,128)(2,1)S(1)} reshape(bf16[32,1024]{1,0:T(8,128)(2,1)} %bitcast.31) | data formatting | bytes 131072 | tf_op jit(solution)/shard_map/reshape | solution.py:185
  9.7 0.1 reshape.51
  9.8 17.1 %all_to_all.15 = bf16[16,2,1024]{2,1,0:T(2,128)(2,1)S(1)} all-to-all(bf16[16,2,1024]{2,1,0:T(2,128)(2,1)S(1)} %reshape.51), channel_id=1, replica_groups=mesh['perm'=16,'summa'=32] {'perm'}, dimensions={0} | all-to-all | bytes 131072 | tf_op jit(solution)/shard_map/all_to_all | solution.py:186
  27.0 0.1 reshape.52
  27.1 0.1 pad_maximum_fusion.1
  27.2 0.9 %broadcast_in_dim.6 = bf16[8,8,32,128]{3,2,1,0:T(8,128)(2,1)} broadcast(bf16[8,32,128]{2,1,0:T(8,128)(2,1)S(1)} %pad_maximum_fusion.1), dimensions={1,2,3} | broadcast | bytes 589824 | tf_op jit(solution)/shard_map/broadcast_in_dim | solution.py:18
  28.1 11.3 %all-to-all-start.1 = ((bf16[8,8,32,128]{3,2,1,0:T(8,128)(2,1)}), bf16[8,8,32,128]{3,2,1,0:T(8,128)(2,1)S(1)}, u32[]{:S(2)}, u32[]{:S(2)}) async-start(bf16[8,8,32,128]{3,2,1,0:T(8,128)(2,1)} %broadcast_in_dim.6), calls=%async_computation.1 | async-start | bytes 1048576 | tf_op jit(solution)/shard_map/all_to_all | solution.py:19
  39.4 0.7 or_and_fusion
  40.1 0.7 fusion
  48.1 2.8 %all-to-all-done.1 = bf16[8,8,32,128]{3,2,1,0:T(8,128)(2,1)S(1)} async-done(((bf16[8,8,32,128]{3,2,1,0:T(8,128)(2,1)}), bf16[8,8,32,128]{3,2,1,0:T(8,128)(2,1)S(1)}, u32[]{:S(2)}, u32[]{:S(2)}) %all-to-all-start.1) | async-done | bytes 524320 | tf_op jit(solution)/shard_map/all_to_all | solution.py:19
  50.9 1.2 %broadcast_in_dim.7 = bf16[4,4,8,32,128]{4,3,2,1,0:T(8,128)(2,1)} broadcast(bf16[4,8,32,128]{3,2,1,0:T(8,128)(2,1)S(1)} %pad_maximum_fusion), dimensions={1,2,3,4} | broadcast | bytes 1310720 | tf_op jit(solution)/shard_map/broadcast_in_dim | solution.py:18
  52.1 6.0 %all-to-all-start.2 = ((bf16[4,4,8,32,128]{4,3,2,1,0:T(8,128)(2,1)}), bf16[4,4,8,32,128]{4,3,2,1,0:T(8,128)(2,1)S(1)}, u32[]{:S(2)}, u32[]{:S(2)}) async-start(bf16[4,4,8,32,128]{4,3,2,1,0:T(8,128)(2,1)} %broadcast_in_dim.7), calls=%async_computation.2 | async-start | bytes 2097152 | tf_op jit(solution)/shard_map/all_to_all | solution.py:19
  58.1 0.0 copy-done.2
  58.1 0.1 reshape.45.mask
  58.2 0.0 copy-done.3
  58.2 0.1 dynamic_slice.20
  58.3 0.1 sub.38
  58.3 0.1 sub.39
  58.4 0.0 copy-done.4
  58.5 0.1 sub.41
  58.6 0.0 copy-done.5
  58.6 0.1 broadcast_subtract_fusion.col_energy
  58.6 10.9 %all-to-all-done.2.tiles = bf16[4,4,8,32,128]{4,3,2,1,0:T(8,128)(2,1)S(1)} async-done(((bf16[4,4,8,32,128]{4,3,2,1,0:T(8,128)(2,1)}), bf16[4,4,8,32,128]{4,3,2,1,0:T(8,128)(2,1)S(1)}, u32[]{:S(2)}, u32[]{:S(2)}) %all-to-all-start.2) | async-done | bytes 1048608 | tf_op jit(solution)/shard_map/all_to_all | solution.py:19
  69.6 0.1 broadcast_in_dim.8.row_energy
  69.7 2.1 %shard_map.82.lhs = bf16[512,1024]{1,0:T(8,128)(2,1)S(1)} custom-call(s32[1024]{0:T(1024)S(1)} %reshape.45.mask, s32[4]{0:T(128)S(1)} %copy-done, s32[1]{0:T(128)} %bitcast.row_tile, bf16[4,4,8,32,128]{4,3,2,1,0:T(8,128)(2,1)S(1)} %all-to-all-done.2.tiles), custom_call_target="tpu_custom_call" | custom-call | tf_op jit(solution)/shard_map/pallas_call | solution.py:52
  71.8 1.9 %all-gather.3.cloned.1.call-done = bf16[32,128,1024]{2,1,0:T(8,128)(2,1)} async-done(((bf16[2,128,1024]{2,1,0:T(8,128)(2,1)}), bf16[32,128,1024]{2,1,0:T(8,128)(2,1)}) %all-gather.3.cloned.1.call-update) | async-done | bytes 8388624 | tf_op jit(solution)/shard_map/all_gather | solution.py:183
  73.7 0.0 copy-done.1
  73.7 7.2 %shard_map.83 = bf16[512,2,1024]{2,1,0:T(2,128)(2,1)} custom-call(s32[16]{0:T(128)S(1)} %copy-done.1, s32[4]{0:T(128)S(1)} %copy-done, bf16[512,1024]{1,0:T(8,128)(2,1)S(1)} %shard_map.82.lhs, f32[512,128]{1,0:T(8,128)S(1)} %broadcast_in_dim.8.row_energy, f32[2,1024]{1,0:T(2,128)S(1)} %broadcast_subtract_fusion.col_energy, bf16[16,2,128,1024]{3,2,1,0:T(8,128)(2,1)} %bitcast.27), custom_call_target="tpu_custom_call" | custom-call | tf_op jit(solution)/shard_map/pallas_call | solution.py:143
  (12 shorter events, 0.1 us)
Async XLA Ops:
  6.5 51.9 %copy-start.4 = (f32[8]{0:T(128)S(1)}, f32[8]{0:T(128)}, u32[]{:S(2)}) copy-start(f32[8]{0:T(128)} %param.14) | copy-start | bytes 100
  6.5 51.6 %copy-start.3 = (f32[1024]{0:T(1024)S(1)}, f32[1024]{0:T(1024)}, u32[]{:S(2)}) copy-start(f32[1024]{0:T(1024)} %param.13) | copy-start | bytes 12292
  6.5 63.2 %copy-start = (s32[4]{0:T(128)S(1)}, s32[4]{0:T(128)}, u32[]{:S(2)}) copy-start(s32[4]{0:T(128)} %window.3) | copy-start | bytes 52
  6.5 51.5 %copy-start.2 = (s32[8,2,8,8]{3,2,1,0:T(8,128)S(1)}, s32[8,2,8,8]{3,2,1,0:T(8,128)}, u32[]{:S(2)}) copy-start(s32[8,2,8,8]{3,2,1,0:T(8,128)} %param.10) | copy-start | bytes 12292
  6.5 52.0 %copy-start.5 = (f32[2]{0:T(128)S(1)}, f32[2]{0:T(128)}, u32[]{:S(2)}) copy-start(f32[2]{0:T(128)} %param.15) | copy-start | bytes 28
  6.5 67.1 %copy-start.1 = (s32[16]{0:T(128)S(1)}, s32[16]{0:T(128)}, u32[]{:S(2)}) copy-start(s32[16]{0:T(128)} %panel_slot.1) | copy-start | bytes 196
  6.6 67.1 %all-gather.3.cloned.1.call-start = ((), (), s32[]{:S(2)}) async-start(), calls=%async_computation.3 | async-start | bytes 8912896 | tf_op jit(solution)/shard_map/all_gather | solution.py:183
  28.1 22.8 %all-to-all-start.1 = ((bf16[8,8,32,128]{3,2,1,0:T(8,128)(2,1)}), bf16[8,8,32,128]{3,2,1,0:T(8,128)(2,1)S(1)}, u32[]{:S(2)}, u32[]{:S(2)}) async-start(bf16[8,8,32,128]{3,2,1,0:T(8,128)(2,1)} %broadcast_in_dim.6), calls=%async_computation.1 | async-start | bytes 1048576 | tf_op jit(solution)/shard_map/all_to_all | solution.py:19
  52.1 17.5 %all-to-all-start.2 = ((bf16[4,4,8,32,128]{4,3,2,1,0:T(8,128)(2,1)}), bf16[4,4,8,32,128]{4,3,2,1,0:T(8,128)(2,1)S(1)}, u32[]{:S(2)}, u32[]{:S(2)}) async-start(bf16[4,4,8,32,128]{4,3,2,1,0:T(8,128)(2,1)} %broadcast_in_dim.7), calls=%async_computation.2 | async-start | bytes 2097152 | tf_op jit(solution)/shard_map/all_to_all | solution.py:19
Sparse Core Ops, SparseCore 0:
  9.5 64.1 all-gather.2
